TPU v7x, 32 devices: a whole 2x2x4 slice. The times are simulated.
32 devices in a mesh: dp: 4 (over y, core), blk: 8 (over z, x).
Axes of the slice: x: 2, y: 2, z: 4, core: 2. Of those that a mesh axis runs over, the one named last changes fastest.
Arguments:
- inputs: bfloat16 [4, 4, 1024, 768], P(None, 'dp', 'blk'), may hold values from -6 to 6
- segment_ids: int32 [4, 4, 1024], P(None, 'dp', 'blk'), may hold values from 0 to 1023, as said below
- query_weight: bfloat16 [768, 768], P('dp', 'blk'), may hold values from -0.21875 to 0.21875
- query_bias: bfloat16 [768], P('blk'), may hold values from -3 to 3
- key_weight: bfloat16 [768, 768], P('dp', 'blk'), may hold values from -0.21875 to 0.21875
- value_weight: bfloat16 [768, 768], P('dp', 'blk'), may hold values from -0.21875 to 0.21875
- value_bias: bfloat16 [768], P('blk'), may hold values from -3 to 3
- output_weight: bfloat16 [768, 768], P('dp', 'blk'), may hold values from -1.25 to 1.25
- output_bias: bfloat16 [768], P('blk'), may hold values from -3 to 3
- first_gain: bfloat16 [768], P('blk'), may hold values from 0.5 to 1.5
- first_shift: bfloat16 [768], P('blk'), may hold values from -3 to 3
- up_weight: bfloat16 [768, 3072], P('dp', 'blk'), may hold values from -0.21875 to 0.21875
- up_bias: bfloat16 [3072], P('blk'), may hold values from -3 to 3
- down_weight: bfloat16 [3072, 768], P('dp', 'blk'), may hold values from -0.109375 to 0.109375
- down_bias: bfloat16 [768], P('blk'), may hold values from -3 to 3
- second_gain: bfloat16 [768], P('blk'), may hold values from 0.5 to 1.5
- second_shift: bfloat16 [768], P('blk'), may hold values from -3 to 3
- cotangent: bfloat16 [4, 4, 1024, 768], P(None, 'dp', 'blk'), may hold values from -6 to 6
Outputs:
- layer_output: bfloat16 [4, 4, 1024, 768], P(None, 'dp', 'blk')
- input_grad: bfloat16 [4, 4, 1024, 768], P(None, 'dp', 'blk')
- grad_query_weight: float32 [768, 768], P('dp', 'blk')
- grad_query_bias: float32 [768], P('blk')
- grad_key_weight: float32 [768, 768], P('dp', 'blk')
- grad_value_weight: float32 [768, 768], P('dp', 'blk')
- grad_value_bias: float32 [768], P('blk')
- grad_output_weight: float32 [768, 768], P('dp', 'blk')
- grad_output_bias: float32 [768], P('blk')
- grad_first_gain: float32 [768], P('blk')
- grad_first_shift: float32 [768], P('blk')
- grad_up_weight: float32 [768, 3072], P('dp', 'blk')
- grad_up_bias: float32 [3072], P('blk')
- grad_down_weight: float32 [3072, 768], P('dp', 'blk')
- grad_down_bias: float32 [768], P('blk')
- grad_second_gain: float32 [768], P('blk')
- grad_second_shift: float32 [768], P('blk')
Inputs may be any that keep to these rules, and one draw needn't show every extreme that they name: `segment_ids`: along each row the ids never fall, and a passage is a run of equal ids. The last passage of every row has id 1024 - 1, and every other passage has a smaller id. Among the rows of one index of dp (all micro-batches), one row holds a passage that begins among the first 128 positions and ends among the last 128.
All inputs are finite; a program needn't handle non-finite values.
Results may differ from a plain program's by a relative error of at most 0.019.
Values may be sent and summed in bfloat16 or wider, within the bound.
A program may use at most 256 MiB of HBM per device.

v0:
```python
from functools import partial

import jax
import jax.numpy as jnp
from jax import lax
from jax.experimental import pallas as pl
from jax.experimental.pallas import tpu as pltpu
from jax.sharding import PartitionSpec as P

MESH = pl.DeviceIdType.MESH
BF = jnp.bfloat16
F32 = jnp.float32


(BEGIN, RELAY, TOKENS, BLOCK, OTHER, COTANGENT, PAIR, QUERY, KEY, VALUE, HEAD, BRANCH, UP, DOWN) = range(14)
(LAUNCH, ABSORB, HOME, GRAD_U, GRAD_D, GRAD_T, HEAD_BACK, EXCHANGE, MERGE, INPUT_GRAD, VECTORS, VECTORS_LAST) = range(14, 26)


def place():
    dp = lax.axis_index("dp")
    blk = lax.axis_index("blk")
    return dp // 2, dp % 2, blk // 2, blk % 2


def device(y, c, z, x):
    return (y * 2 + c, z * 2 + x)


def greet_all():
    y, c, z, x = place()
    me = (y * 2 + c) * 8 + z * 2 + x
    barrier = pltpu.get_barrier_semaphore()

    def greet(i, carry):
        other = (me + i) % 32
        pl.semaphore_signal(barrier, inc=1, device_id=(other // 8, other % 8), device_id_type=MESH)
        return carry

    lax.fori_loop(1, 32, greet, 0)
    return lambda: pl.semaphore_wait(barrier, 31)


def coords():
    y, c, z, x = place()
    return {"a": z // 2, "b": z % 2, "x": x, "y": y, "c": c}


def to_device(at):
    return device(at["y"], at["c"], 2 * at["a"] + at["b"], at["x"])


def flip(at, dim):
    return {**at, dim: 1 - at[dim]}


def whole(at, dims):
    return {k: (None if k in dims else v) for k, v in at.items()}


def span(v):
    return slice(None) if v is None else v


def each(v):
    return (0, 1) if v is None else (v,)


def lanes(start, size):
    return pl.ds(start if isinstance(start, int) else pl.multiple_of(start, 128), size)


def region(refs, chunk, at):
    wt, wu, wd = refs
    kind, i, _ = chunk
    a, b, x, y, c = (at[k] for k in "abxyc")
    if kind == "t":
        cols = slice(None) if y is None else lanes(384 * y, 384)
        return [wt.at[i, span(a), span(b), span(x), span(c), :, cols]]
    if kind == "u":
        if a is None and b is None and x is None:
            return [wu.at[span(y), span(c), i]]
        return [wu.at[span(y), span(c), i, :, lanes(384 * (4 * p + 2 * q + r), 384)] for p in each(a) for q in each(b) for r in each(x)]
    return [wd.at[span(a), span(b), span(x), i // 2, :, lanes(768 * (2 * p + q) + 384 * (i % 2), 384)] for p in each(y) for q in each(c)]


HEADS, HD = 12, 64
NT = (((1,), (1,)), ((), ()))
NN = (((1,), (0,)), ((), ()))


def dot(l, r, dims=NN):
    return lax.dot_general(l, r, dims, preferred_element_type=F32)


VM = pl.BlockSpec(memory_space=pltpu.VMEM)
ANY = pl.BlockSpec(memory_space=pl.ANY)


def sds(shape, dt=BF):
    return jax.ShapeDtypeStruct(shape, dt)


def norm(h):
    centred = h - jnp.mean(h, axis=-1, keepdims=True)
    inv = lax.rsqrt(jnp.mean(centred * centred, axis=-1, keepdims=True) + 1e-12)
    return centred * inv, inv


def norm_back(g, normed, inv):
    return inv * (g - jnp.mean(g, axis=-1, keepdims=True) - normed * jnp.mean(g * normed, axis=-1, keepdims=True))


FORWARD_CHUNKS = (
    ("t", 0, "abxyc"), ("t", 1, "abxyc"), ("t", 2, "abyxc"), ("t", 3, "abxyc"), ("u", 0, "abxyc"), ("u", 1, "abyxc"), ("u", 2, "abxyc"),
    ("u", 3, "axbyc"), ("d", 0, "abyxc"), ("d", 2, "abxyc"), ("d", 1, "abyxc"), ("d", 3, "abxyc"),
)
FORWARD_PLAN = (
    (TOKENS, 0), (PAIR,), (BEGIN, 0), (BEGIN, 1), (RELAY, 0, 0), (BEGIN, 2), (TOKENS, 1), (RELAY, 1, 0), (BEGIN, 3), (RELAY, 0, 1),
    (RELAY, 2, 0), (BEGIN, 4), (RELAY, 1, 1), (RELAY, 0, 2), (RELAY, 2, 1), (RELAY, 3, 0), (BEGIN, 5), (TOKENS, 2), (RELAY, 4, 0),
    (BEGIN, 6), (RELAY, 1, 2), (RELAY, 3, 1), (RELAY, 0, 3), (RELAY, 5, 0), (BEGIN, 7), (RELAY, 0, 4), (RELAY, 2, 2), (RELAY, 4, 1),
    (RELAY, 3, 2), (RELAY, 1, 3), (RELAY, 5, 1), (RELAY, 6, 0), (BEGIN, 8), (TOKENS, 3), (BLOCK, 0), (BLOCK, 1), (RELAY, 1, 4),
    (RELAY, 2, 3), (OTHER, 0), (BLOCK, 2), (RELAY, 7, 0), (BEGIN, 9), (OTHER, 1), (RELAY, 2, 4), (RELAY, 6, 1), (OTHER, 2), (RELAY, 4, 2),
    (RELAY, 8, 0), (BEGIN, 10), (RELAY, 3, 3), (RELAY, 3, 4), (RELAY, 5, 2), (RELAY, 7, 1), (RELAY, 8, 1), (RELAY, 9, 0), (RELAY, 6, 2),
    (BEGIN, 11), (COTANGENT, 0), (COTANGENT, 1), (COTANGENT, 2), (COTANGENT, 3), (RELAY, 10, 0), (BLOCK, 3), (QUERY,), (RELAY, 4, 3),
    (RELAY, 5, 3), (RELAY, 7, 2), (OTHER, 3), (KEY,), (RELAY, 4, 4), (RELAY, 5, 4), (RELAY, 9, 1), (VALUE,), (RELAY, 8, 2), (RELAY, 11, 0),
    (HEAD, 0), (HEAD, 1), (RELAY, 6, 3), (HEAD, 2), (HEAD, 3), (RELAY, 6, 4), (RELAY, 7, 3), (HEAD, 4), (HEAD, 5), (RELAY, 7, 4),
    (HEAD, 6), (HEAD, 7), (HEAD, 8), (HEAD, 9), (RELAY, 9, 2), (RELAY, 10, 1), (HEAD, 10), (RELAY, 11, 1), (HEAD, 11), (RELAY, 8, 3),
    (BRANCH,), (RELAY, 8, 4), (RELAY, 9, 3), (UP, 0), (RELAY, 9, 4), (UP, 1), (RELAY, 10, 2), (RELAY, 11, 2), (UP, 2), (UP, 3), (DOWN, 0),
    (RELAY, 10, 3), (RELAY, 11, 3), (RELAY, 10, 4), (RELAY, 11, 4), (DOWN, 1),
)
BACKWARD_CHUNKS = (
    ("d", 3, "bxayc"), ("d", 0, "axbyc"), ("u", 3, "axybc"), ("d", 1, "abyxc"), ("d", 2, "aybxc"), ("u", 1, "bxayc"), ("u", 2, "baxyc"),
    ("t", 3, "aybxc"), ("u", 0, "baxyc"), ("t", 0, "abxyc"), ("t", 1, "baxyc"), ("t", 2, "axbyc"),
)
BACKWARD_PLAN = (
    (GRAD_D, 3), (LAUNCH, 0), (GRAD_D, 0), (LAUNCH, 1), (HOME, 0), (HOME, 1), (HOME, 2), (HEAD_BACK, 0), (ABSORB, 0, 0), (GRAD_U, 3),
    (LAUNCH, 2), (ABSORB, 1, 0), (GRAD_D, 1), (LAUNCH, 3), (HOME, 3), (HEAD_BACK, 1), (ABSORB, 2, 0), (GRAD_D, 2), (LAUNCH, 4),
    (ABSORB, 0, 1), (ABSORB, 3, 0), (GRAD_U, 1), (LAUNCH, 5), (HEAD_BACK, 2), (ABSORB, 4, 0), (GRAD_U, 2), (LAUNCH, 6), (ABSORB, 1, 1),
    (ABSORB, 5, 0), (GRAD_T, 3), (LAUNCH, 7), (HEAD_BACK, 3), (ABSORB, 6, 0), (GRAD_U, 0), (LAUNCH, 8), (ABSORB, 3, 1), (ABSORB, 7, 0),
    (ABSORB, 2, 1), (ABSORB, 5, 1), (HEAD_BACK, 4), (ABSORB, 8, 0), (HEAD_BACK, 5), (HEAD_BACK, 6), (ABSORB, 4, 1), (ABSORB, 6, 1),
    (HEAD_BACK, 7), (HEAD_BACK, 8), (ABSORB, 0, 2), (ABSORB, 1, 2), (HEAD_BACK, 9), (ABSORB, 3, 2), (ABSORB, 7, 1), (HEAD_BACK, 10),
    (HEAD_BACK, 11), (EXCHANGE,), (ABSORB, 2, 2), (ABSORB, 4, 2), (ABSORB, 3, 3), (ABSORB, 5, 2), (ABSORB, 6, 2), (ABSORB, 8, 1),
    (ABSORB, 0, 3), (ABSORB, 7, 2), (ABSORB, 1, 3), (MERGE,), (GRAD_T, 0), (LAUNCH, 9), (ABSORB, 2, 3), (ABSORB, 3, 4), (GRAD_T, 1),
    (LAUNCH, 10), (ABSORB, 0, 4), (ABSORB, 4, 3), (ABSORB, 5, 3), (INPUT_GRAD,), (ABSORB, 6, 3), (ABSORB, 1, 4), (ABSORB, 7, 3),
    (ABSORB, 8, 2), (ABSORB, 9, 0), (ABSORB, 10, 0), (ABSORB, 2, 4), (GRAD_T, 2), (LAUNCH, 11), (ABSORB, 5, 4), (ABSORB, 4, 4),
    (ABSORB, 11, 0), (ABSORB, 9, 1), (ABSORB, 10, 1), (ABSORB, 6, 4), (ABSORB, 11, 1), (ABSORB, 9, 2), (ABSORB, 7, 4), (ABSORB, 10, 2),
    (ABSORB, 8, 3), (VECTORS,), (ABSORB, 11, 2), (ABSORB, 9, 3), (ABSORB, 8, 4), (ABSORB, 11, 3), (ABSORB, 10, 3), (ABSORB, 9, 4),
    (ABSORB, 10, 4), (ABSORB, 11, 4), (VECTORS_LAST,),
)
FORWARD = (FORWARD_PLAN, FORWARD_CHUNKS)
BACKWARD = (BACKWARD_PLAN, BACKWARD_CHUNKS)


S = pltpu.SemaphoreType.DMA
FC = 768


def total(v):
    return jnp.sum(v, axis=0, keepdims=True)


class Copies:
    def __init__(self):
        self.sent = []

    def start(self, describe, cond=None):
        def act(method):
            def run():
                src, dst, send, recv, to = describe()
                cp = pltpu.make_async_remote_copy(src_ref=src, dst_ref=dst, send_sem=send, recv_sem=recv, device_id=to, device_id_type=MESH)
                getattr(cp, method)()

            if cond is None:
                run()
            else:
                pl.when(cond())(run)

        act("start")
        self.sent.append(act)

    def start_or_keep(self, mine, describe, local):
        self.start(describe, lambda: jnp.logical_not(mine()))
        src, dst, *_ = describe()
        pl.when(mine())(pltpu.make_async_copy(src, dst, local).start)

    def arrive_or_keep(self, mine, dst, recv, local):
        pl.when(jnp.logical_not(mine))(lambda: arrive(dst, recv))
        pl.when(mine)(pltpu.make_async_copy(dst, dst, local).wait)

    def finish(self):
        for act in self.sent:
            act("wait_send")


def run_plan(plan, work, loops):
    def run(steps):
        for step, *args in steps:
            work[step](*args)

    kinds = [step[0] for step in plan]
    done = 0
    for kind, group in loops:
        first = kinds.index(kind)
        spots = [n for n, other in enumerate(kinds) if other == kind]
        run(plan[done:first])
        between = [plan[n + 1 : m] for n, m in zip(spots, spots[1:])] + [()]

        def body(turn, carry, kind=kind, group=group, between=between):
            for part in range(group):
                work[kind](turn, part)
                for n in range(part, len(between), group):
                    if between[n]:
                        pl.when(turn == n // group)(partial(run, between[n]))
            return carry

        lax.fori_loop(0, len(spots) // group, body, 0)
        done = spots[-1] + 1
    run(plan[done:])


def arrive(dst, recv):
    y, c, z, x = place()
    pltpu.make_async_remote_copy(src_ref=dst, dst_ref=dst, send_sem=recv, recv_sem=recv, device_id=device(y, c, z, x), device_id_type=MESH).wait_recv()


def forward_kernel(
    plan, chunks,
    xs, cot, seg, qw, kw, vw, ow, wup, wdt, small, upb,
    OUT, GF, GC, GST, LOWT, CTX, HID, GI, XO, Q, KT, V, E, CT, RS, WQ, VS,
    wt, wu, wd, pair_src, pair_dst, stage, xbuf, cbuf, sbuf, vec, vbuf, vb, ub,
    qb, kb, ktb, vb_, vtb, mask, ebuf, ctb, rsb, vsb, hid, gib, ctxb, n1, first, acc, rowbuf, outb, gsb, lowb, gcb, gsn,
    ps, pr, ws, wr, ls, xsnd, xrcv, fsnd, frcv, csnd, crcv, ssnd, srcv, vsnd, vrcv, lsem, osem, esem,
):
    y, c, z, x = place()
    j = 2 * z + x
    at = coords()
    partner = device(y, 1 - c, z, x)
    refs = (wt, wu, wd)
    copies = Copies()
    outs = []

    def put(src, dst):
        cp = pltpu.make_async_copy(src, dst, osem.at[len(outs)])
        cp.start()
        outs.append(cp)

    for i, w in enumerate((qw, kw, vw, ow)):
        pair_src[i] = w[...].astype(F32).T.astype(BF)
    vec[...] = jnp.zeros_like(vec)
    vec[0:8, 0:96] = small[...].astype(F32)
    vec[8:11, :] = upb[...].astype(F32)
    greet_all()()
    copies.start(lambda: (pair_src.at[:, pl.ds(48 * (1 - c), 48)], pair_dst, ps, pr, partner))

    def home(b):
        return (b // 2 == z) & (b % 2 == x) & (c == x)

    def send_tokens(src, dst, i, send, recv, local):
        def mine():
            return (z == (z + i) % 4) & (x == c) & (z // 2 == c)

        copies.start_or_keep(mine, lambda: (src.at[(z + i) % 4], dst.at[j % dst.shape[0]], send, recv.at[j % 4], device(y, z // 2, (z + i) % 4, c)), local)

    for i in range(4):
        for k in range(2):
            m = (z + i) % 4
            mine = (z == m) & (x == c) & (k == c)
            copies.start_or_keep(lambda v=mine: v, lambda m=m, i=i, k=k: (seg.at[m], sbuf.at[j], ssnd.at[2 * i + k], srcv.at[j], device(y, k, m, c)), lsem.at[1])
    pltpu.make_async_copy(vec, vbuf.at[j], lsem.at[2]).start()
    for d in range(1, 8):
        o = (j + d) % 8
        copies.start(lambda o=o, d=d: (vec, vbuf.at[j], vsnd.at[d], vrcv.at[d], device(y, c, o // 2, o % 2)))

    def pair_up():
        arrive(pair_dst, pr)
        own = pair_src[:, pl.ds(pl.multiple_of(48 * c, 16), 48), :]
        got = pair_dst[...]
        stage[...] = jnp.concatenate([jnp.where(c == 0, own, got), jnp.where(c == 0, got, own)], axis=-1)

    def source(ch):
        kind, i, _ = ch
        if kind == "t":
            return stage.at[i]
        if kind == "u":
            return wup.at[i]
        return wdt.at[i // 2, :, pl.ds(384 * (i % 2), 384)]

    def begin(u):
        ch = chunks[u]
        here = region(refs, ch, at)[0]
        pltpu.make_async_copy(source(ch), here, ls.at[u]).start()
        copies.start(lambda: (source(ch), region(refs, ch, at)[0], ws.at[u, 0, 0], wr.at[u, 0, 0], to_device(flip(at, ch[2][0]))))

    def relay(u, s):
        ch = chunks[u]
        order = ch[2]
        if s == 0:
            pltpu.make_async_copy(source(ch), region(refs, ch, at)[0], ls.at[u]).wait()

        def parts(at, s):
            if s < 3:
                return [region(refs, ch, whole(at, order[:s]))]
            return [region(refs, ch, whole(v, order[: s - 1])) for v in (at, flip(at, order[s - 1]))]

        def forward(s, h):
            def describe(k):
                part = parts(at, s)[h][k]
                return part, part, ws.at[u, s, 4 * h + k], wr.at[u, s, 4 * h + k], to_device(flip(at, order[s]))

            for k in range(len(parts(at, s)[h])):
                copies.start(partial(describe, k))

        for h, half in enumerate(parts(flip(at, order[s]), s)):
            for k, part in enumerate(half):
                arrive(part, wr.at[u, s, 4 * h + k])
        if s == 0:
            forward(1, 0)
        elif s == 1:
            forward(2, 0)
            forward(3, 0)
        elif s == 2:
            forward(3, 1)
            forward(4, 0)
        elif s == 3:
            forward(4, 1)

    def token_block(i):
        b = 4 * c + i
        copies.arrive_or_keep(home(b), xbuf.at[b], xrcv.at[i], lsem.at[0])
        copies.start(lambda: (xbuf.at[4 * c + i], xbuf.at[4 * c + i], fsnd.at[i], frcv.at[i], partner))

    def weight(i):
        return wt[i].reshape(768, 768)

    ready = []

    def vectors():
        if ready:
            return
        ready.append(True)
        pltpu.make_async_copy(vec, vbuf.at[j], lsem.at[2]).wait()
        for d in range(1, 8):
            arrive(vbuf.at[(j - d) % 8], vrcv.at[d])
        for b in range(8):
            copies.arrive_or_keep(home(b), sbuf.at[b], srcv.at[b], lsem.at[1])
        pieces = [vbuf[b] for b in range(8)]
        vb[...] = jnp.concatenate([p[:8, :96] for p in pieces], axis=-1)
        ub[...] = jnp.concatenate([p[8 + k : 9 + k, :] for p in pieces for k in range(3)], axis=-1)
        row = jnp.concatenate([sbuf[b] for b in range(8)], axis=-1).astype(F32)
        mine = jnp.concatenate([sbuf[4 * c + b] for b in range(4)], axis=-1).astype(F32)
        col = jnp.broadcast_to(row, (8, 1024)).T[:, :1]
        mask[...] = jnp.where(col == mine, 0.0, -1e30)

    def own_rows():
        return xbuf[pl.ds(4 * c, 4)].reshape(512, 768)

    def queries():
        vectors()
        put(xbuf.at[pl.ds(4 * c, 4)], XO)
        q = dot(own_rows(), weight(0), NT) + vb[0:1]
        qb[...] = (q.astype(BF).astype(F32) * 0.125).astype(BF)
        put(qb, Q)

    def keys():
        k = dot(xbuf[...].reshape(1024, 768), weight(1), NT)
        kb[...] = k.astype(BF)
        ktb[...] = k.T.astype(BF)
        put(ktb, KT)

    def values():
        vectors()
        v = dot(xbuf[...].reshape(1024, 768), weight(2), NT) + vb[1:2]
        vb_[...] = v.astype(BF)
        vtb[...] = v.T.astype(BF)
        put(vb_, V)

    def head(p, i):
        h = 2 * p + i
        cols = lanes(128 * p, 128)
        half = lax.broadcasted_iota(jnp.int32, (512, 128), 1) // 64
        qp = qb[:, cols]
        s = dot(kb[:, cols], jnp.where(half == i, qp, jnp.zeros_like(qp)), NT) + mask[...]
        e = jnp.exp(s - jnp.max(s, axis=0, keepdims=True))
        r = 1.0 / jnp.sum(e, axis=0, keepdims=True)
        pl.when(p > 0)(pltpu.make_async_copy(ebuf.at[i], E.at[h], esem.at[i]).wait)
        ebuf[i] = e.astype(BF)
        pltpu.make_async_copy(ebuf.at[i], E.at[h], esem.at[i]).start()
        rsb[pl.ds(h, 1), :] = r
        rows = pl.ds(pl.multiple_of(64 * h, 64), 64)
        ctb[rows, :] = (dot(vtb[rows, :], ebuf[i]) * r).astype(BF)

    def branch():
        put(wt.at[pl.ds(0, 3)], WQ)
        put(ctb, CT)
        put(rsb, RS)
        ctxb[...] = ctb[...].astype(F32).T.astype(BF)
        put(ctxb, CTX)
        normed, inv = norm(own_rows().astype(F32) + dot(ctxb[...], weight(3), NT) + vb[2:3])
        n1[...] = normed
        rowbuf[:, 0:1] = inv
        first[...] = normed * vb[3:4] + vb[4:5]
        lowb[...] = first[...].T.astype(BF)
        put(lowb, LOWT)

    def up(f, _):
        cols = lanes(FC * f, FC)
        inner = dot(first[...].astype(BF), wu[:, :, :, :, cols].reshape(768, FC)) + ub[:, cols]
        cdf = 0.5 * (1.0 + lax.erf(inner * 0.7071067811865476))
        pdf = jnp.exp(-0.5 * inner * inner) * 0.3989422804014327
        hid[:, cols] = (inner * cdf).astype(BF)
        gib[:, cols] = (cdf + inner * pdf).astype(BF)

    downs = []

    def down(b):
        if not downs:
            put(hid, HID)
            acc[...] = first[...] + vb[5:6]

        part = None
        for q in range(4):
            cols = slice(768 * q + 384 * b, 768 * q + 384 * b + 384)
            d = dot(hid[:, cols], wd[:, :, :, :, :, cols].reshape(768, 384), NT)
            part = d if part is None else part + d
        acc[...] += part
        downs.append(b)

    def second_norm():
        normed, inv = norm(acc[...])
        gain = vb[6:7]
        outb[...] = (normed * gain + vb[7:8]).astype(BF)
        put(outb, OUT)
        for b in range(4):
            copies.arrive_or_keep(home(4 * c + b), cbuf.at[b], crcv.at[b], lsem.at[3])
        g = cbuf[...].reshape(512, 768).astype(F32)
        vsb[...] = jnp.zeros_like(vsb)
        vsb[6:7, :768] = total(g * normed)
        vsb[7:8, :768] = total(g)
        gss = norm_back(g * gain, normed, inv)
        gs = gss.astype(BF)
        vsb[5:6, :768] = total(gs.astype(F32))
        acc[...] = gss
        gsb[...] = gss.T.astype(BF)
        put(gsb, GST)
        return gs

    def back(gs):
        gsn[...] = gs

        def step(f, carry):
            cols = lanes(FC * f, FC)
            gi = (dot(gsn[...], wd[:, :, :, :, :, cols].reshape(768, FC)) * gib[:, cols].astype(F32)).astype(BF)
            gib[:, cols] = gi
            vsb[8:9, cols] = total(gi.astype(F32))
            acc[...] += dot(gi, wu[:, :, :, :, cols].reshape(768, FC), NT)
            return carry

        lax.fori_loop(0, 3072 // FC, step, 0)
        put(gib, GI)
        gf = acc[...]
        vsb[3:4, :768] = total(gf * n1[...])
        vsb[4:5, :768] = total(gf)
        gsf = norm_back(gf * vb[3:4], n1[...], rowbuf[:, 0:1])
        first[...] = gsf
        put(first, GF)
        gb = gsf.astype(BF)
        vsb[2:3, :768] = total(gb.astype(F32))
        VS[...] = vsb[...]
        gcb[...] = dot(gb, weight(3)).astype(BF)
        put(gcb, GC)

    def tokens(i):
        send_tokens(xs, xbuf, i, xsnd.at[i], xrcv, lsem.at[0])

    def cotangent(i):
        send_tokens(cot, cbuf, i, csnd.at[i], crcv, lsem.at[3])

    def other_block(i):
        arrive(xbuf.at[4 * (1 - c) + i], frcv.at[i])

    work = {
        BEGIN: begin, RELAY: relay, TOKENS: tokens, BLOCK: token_block, OTHER: other_block, COTANGENT: cotangent, PAIR: pair_up,
        QUERY: queries, KEY: keys, VALUE: values, HEAD: head, BRANCH: branch, UP: up, DOWN: down,
    }
    run_plan(plan, work, ((HEAD, 2), (UP, 1)))
    back(second_norm())
    for i in range(2):
        pltpu.make_async_copy(ebuf.at[i], E.at[10 + i], esem.at[i]).wait()
    for cp in outs:
        cp.wait()
    copies.finish()


def forward_call(plan, chunks, xs, cot, seg, qw, kw, vw, ow, wup, wdt, small, upb):
    n = len(chunks)
    V_ = pltpu.VMEM
    row = (512, 768)
    return pl.pallas_call(
        partial(forward_kernel, plan, chunks),
        out_shape=[
            sds(row), sds(row, F32), sds(row), sds((768, 512)), sds((768, 512)), sds(row), sds((512, 3072)), sds((512, 3072)),
            sds((4, 128, 768)), sds(row), sds((768, 1024)), sds((1024, 768)), sds((12, 1024, 512)), sds((768, 512)), sds((16, 512), F32),
            sds((3, 2, 2, 2, 2, 48, 768)), sds((16, 3072), F32),
        ],
        in_specs=[ANY, ANY] + [VM] * 9,
        out_specs=[ANY] * 16 + [VM],
        scratch_shapes=[
            V_((4, 2, 2, 2, 2, 48, 768), BF), V_((2, 2, 4, 48, 3072), BF), V_((2, 2, 2, 2, 48, 3072), BF),
            V_((4, 96, 192), BF), V_((4, 48, 192), BF), V_((4, 48, 384), BF), V_((8, 128, 768), BF), V_((4, 128, 768), BF),
            V_((8, 1, 128), jnp.int32), V_((16, 128), F32), V_((8, 16, 128), F32), V_((8, 768), F32), V_((1, 3072), F32),
            V_(row, BF), V_((1024, 768), BF), V_((768, 1024), BF), V_((1024, 768), BF), V_((768, 1024), BF), V_((1024, 512), F32),
            V_((2, 1024, 512), BF), V_((768, 512), BF), V_((16, 512), F32), V_((16, 3072), F32), V_((512, 3072), BF), V_((512, 3072), BF),
            V_(row, BF), V_(row, F32), V_(row, F32), V_(row, F32), V_((512, 128), F32), V_(row, BF), V_((768, 512), BF), V_((768, 512), BF), V_(row, BF), V_(row, BF),
            S, S, S((n, 5, 8)), S((n, 5, 8)), S((n,)), S((4,)), S((4,)), S((4,)), S((4,)), S((4,)), S((4,)), S((8,)), S((8,)), S((8,)), S((8,)),
            S((4,)), S((24,)), S((2,)),
        ],
        name="forward",
        compiler_params=pltpu.CompilerParams(collective_id=1, has_side_effects=True, vmem_limit_bytes=59 * 2**20),
    )(xs, cot, seg, qw, kw, vw, ow, wup, wdt, small, upb)


def landing(at, order, s):
    spot = dict(at)
    for d in order[s + 1 :]:
        spot[d] = 1 - at[d]
    return whole(spot, order[:s])


def backward_kernel(
    plan, chunks,
    OUT, GF, GC, GST, LOWT, CTX, HID, GI, XO, Q, KT, V, E, CT, RS, WQ, VS,
    LO, IG, D4, DU, DD, VO,
    gt, gu, gd, rt, ru, rd, hid, gib, gst, lowt, xb, qb, ktb, vb, ctb, gcb, gct, gfb, ebuf,
    dqt, dkb, dvb, dkr, dvr, igb, rcol, vpack, vrecv, vsum, vrecv2, pairs, pairr, fin,
    isem, esem, lsem, ks, kr, os_, or_, gs, gr, vs_, vr, ws, wr, ps, pr,
):
    y, c, z, x = place()
    j = 2 * z + x
    at = coords()
    partner = device(y, 1 - c, z, x)
    G, R = (gt, gu, gd), (rt, ru, rd)
    copies = Copies()
    loads = {}
    for src, dst, name in (
        (GST, gst, "gst"), (HID, hid, "hid"), (LOWT, lowt, "lowt"), (GI, gib, "gi"), (V, vb, "v"), (Q, qb, "q"), (GC, gcb, "gc"), (KT, ktb, "kt"),
        (CT, ctb, "ct"), (CTX, igb, "ctx"), (XO, xb, "x"), (GF, gfb, "gf"),
    ):
        cp = pltpu.make_async_copy(src, dst, isem.at[len(loads)])
        cp.start()
        loads[name] = cp
    for i in range(2):
        pltpu.make_async_copy(E.at[i], ebuf.at[i], esem.at[i]).start()

    def need(*names):
        for n in names:
            if n in loads:
                loads.pop(n).wait()

    all_here = greet_all()

    def send_home(src, out, w, k):
        def mine():
            b = 4 * c + k
            return (x == c) & (b // 2 == z) & (b % 2 == x)

        def describe():
            b = 4 * c + k
            return src.at[pl.ds(128 * k, 128)], out.at[z], os_.at[w, k], or_.at[w, z], device(y, x, b // 2, b % 2)

        copies.start_or_keep(mine, describe, lsem.at[w])

    def send_out(k):
        send_home(OUT, LO, 0, k)

    def send_grad(k):
        send_home(igb, IG, 1, k)

    def halves(order, s, at):
        if s == 3:
            return [flip(at, order[2]), at]
        return [at]

    def stage(ch, s, at, h):
        order = ch[2]
        spot = landing(at, order, s)
        own = whole(at, order[:s])
        if s == 3:
            own[order[2]] = spot[order[2]] = halves(order, s, at)[h][order[2]]
        return region(G, ch, own), region(R, ch, spot)

    def launch(u, s):
        ch = chunks[u]
        to = flip(at, ch[2][s])

        def describe(h, k):
            to = flip(at, ch[2][s])
            src, dst = stage(ch, s, to, h)
            return src[k], dst[k], gs.at[u, s, 4 * h + k], gr.at[u, s, 4 * h + k], to_device(to)

        for h in range(2 if s == 3 else 1):
            for k in range(len(stage(ch, s, to, h)[0])):
                copies.start(partial(describe, h, k))

    def take(u, s, h):
        for k, (own, got) in enumerate(zip(*stage(chunks[u], s, at, h))):
            arrive(got, gr.at[u, s, 4 * h + k])
            own[...] = own[...] + got[...]

    def absorb(u, s):
        kind, i, order = ch = chunks[u]
        if s > 0:
            if s == 2:
                take(u, 3, 1)
            take(u, s, 0)
            launch(u, s - 1)
            return
        (own,), (got,) = stage(ch, 0, at, 0)
        arrive(got, gr.at[u, 0, 0])
        done = own[...].astype(F32) + got[...].astype(F32)
        if kind == "u":
            DU[i] = done
        elif kind == "d":
            DD[i // 2, :, 384 * (i % 2) : 384 * (i % 2) + 384] = done
        else:
            lo, hi = done[:, :192], done[:, 192:]
            fin[i, pl.ds(pl.multiple_of(48 * c, 16), 48), :] = jnp.where(c == 0, lo, hi)
            pairs[i] = jnp.where(c == 0, hi, lo)
            copies.start(lambda: (pairs.at[i], pairr.at[i], ps.at[i], pr.at[i], partner))

    made = []

    def grad_u(i):
        made.append(i)
        need("lowt", "gi")
        rows = lowt[...].reshape(2, 2, 4, 48, 512)[:, :, i].reshape(192, 512)

        def columns(q, carry):
            cols = lanes(768 * q, 768)
            gu[:, :, i, :, cols] = dot(rows, gib[:, cols]).astype(BF).reshape(2, 2, 48, 768)
            return carry

        lax.fori_loop(0, 4, columns, 0)

    def grad_d(i):
        made.append(i)
        need("gst", "hid")
        rows = gst[...].reshape(2, 2, 2, 2, 48, 512)[:, :, :, i // 2].reshape(384, 512)

        def columns(q, carry):
            cols = lanes(768 * q + 384 * (i % 2), 384)
            gd[:, :, :, i // 2, :, cols] = dot(rows, hid[:, cols]).astype(BF).reshape(2, 2, 2, 48, 384)
            return carry

        lax.fori_loop(0, 4, columns, 0)

    shape = (2, 2, 2, 2, 48, 768)

    def grad_t(i):
        if i == 3:
            need("gf", "ctx")
            gt[3] = dot(gfb[...].T.astype(BF), igb[...]).astype(BF).reshape(shape)
        elif i == 0:
            need("x")
            gt[0] = dot(dqt[...], xb[...].reshape(512, 768)).astype(BF).reshape(shape)
        else:
            src = dkr if i == 1 else dvr
            gt[i] = dot(src[...].astype(F32).T.astype(BF), xb[...].reshape(512, 768)).astype(BF).reshape(shape)

    def ready():
        need("gc", "v", "q", "kt", "ct")
        gct[...] = gcb[...].astype(F32).T.astype(BF)
        rcol[...] = RS[...].T

    def head(p, i):
        h = 2 * p + i
        cols = lanes(128 * p, 128)
        rows = pl.ds(pl.multiple_of(64 * h, 64), 64)
        qp = qb[:, cols]
        half = lax.broadcasted_iota(jnp.int32, (512, 128), 1) // 64
        column = lax.broadcasted_iota(jnp.int32, (512, 16), 1)
        scale = jnp.sum(jnp.where(column == h, rcol[...], 0.0), axis=1, keepdims=True)
        gm = jnp.where(half == i, gcb[:, cols].astype(F32) * scale, 0.0).astype(BF)
        qm = jnp.where(half == i, qp, jnp.zeros_like(qp))
        delta = total(ctb[rows, :].astype(F32) * gct[rows, :].astype(F32)) * RS[pl.ds(h, 1), :]
        pltpu.make_async_copy(E.at[h], ebuf.at[i], esem.at[i]).wait()
        ds = (ebuf[i].astype(F32) * (dot(vb[:, cols], gm, NT) - delta)).astype(BF)
        dv = dot(ebuf[i], gm)
        dk = dot(ds, qm)
        dqt[rows, :] = (dot(ktb[rows, :], ds) * 0.125).astype(BF)
        pl.when(p < 5)(pltpu.make_async_copy(E.at[jnp.minimum(h + 2, 11)], ebuf.at[i], esem.at[i]).start)
        dkb[:, cols] = dk.astype(BF) if i == 0 else (dkb[:, cols].astype(F32) + dk).astype(BF)
        dvb[:, cols] = dv.astype(BF) if i == 0 else (dvb[:, cols].astype(F32) + dv).astype(BF)

    theirs = pl.ds(pl.multiple_of(512 * (1 - c), 128), 512)
    ours = pl.ds(pl.multiple_of(512 * c, 128), 512)

    def weight_copies():
        for i in range(3):
            cols = slice(768 * i, 768 * i + 768)
            yield pltpu.make_async_copy(WQ.at[i, pl.ds(0, 512)], hid.at[:, cols], isem.at[13 + 2 * i])
            yield pltpu.make_async_copy(WQ.at[i, pl.ds(512, 256)], gib.at[pl.ds(0, 256), cols], isem.at[14 + 2 * i])

    def exchange():
        assert len(made) == 8
        for cp in weight_copies():
            cp.start()
        copies.start(lambda: (dkb.at[theirs], dkr, ks.at[0], kr.at[0], partner))
        copies.start(lambda: (dvb.at[theirs], dvr, ks.at[1], kr.at[1], partner))

    def merge():
        arrive(dkr, kr.at[0])
        arrive(dvr, kr.at[1])
        dkr[...] = (dkb[ours].astype(F32) + dkr[...].astype(F32)).astype(BF)
        dvr[...] = (dvb[ours].astype(F32) + dvr[...].astype(F32)).astype(BF)

    def token_grads():
        need("gf")
        for cp in weight_copies():
            cp.wait()
        dq = dqt[...].astype(F32).T
        ig = gfb[...]
        for i, g in enumerate((dq.astype(BF), dkr[...], dvr[...])):
            cols = slice(768 * i, 768 * i + 768)
            ig = ig + dot(g[:, :512], hid[:, cols]) + dot(g[:, 512:], gib[:256, cols])
        low = jnp.concatenate([total(dq), total(dvr[...].astype(F32)), VS[2:8, :768]], axis=0)
        vpack[...] = jnp.zeros_like(vpack)
        for b in range(8):
            vpack[b, 0:8, 0:96] = low[:, 96 * b : 96 * b + 96]
            vpack[b, 8:9, :] = VS[8:9, 384 * b : 384 * b + 384]
        for d in range(1, 8):
            o = (j + d) % 8
            copies.start(lambda o=o, d=d: (vpack.at[o], vrecv.at[d], vs_.at[d], vr.at[d], device(y, c, o // 2, o % 2)))
        igb[...] = ig.astype(BF)
        for k in range(4):
            send_grad(k)

    def vectors_first():
        acc = vpack[j]
        for d in range(1, 8):
            arrive(vrecv.at[d], vr.at[d])
            acc = acc + vrecv[d]
        vsum[...] = acc
        me = 2 * y + c
        for d in range(1, 4):
            copies.start(lambda d=d: (vsum, vrecv2.at[d], ws.at[d], wr.at[d], ((me + d) % 4, j)))

    def vectors_last():
        acc = vsum[...]
        for d in range(1, 4):
            arrive(vrecv2.at[d], wr.at[d])
            acc = acc + vrecv2[d]
        VO[...] = acc

    work = {
        LAUNCH: lambda u: launch(u, 4), ABSORB: lambda u, s: absorb(u, 4 - s), HOME: send_out, GRAD_U: grad_u, GRAD_D: grad_d, GRAD_T: grad_t,
        HEAD_BACK: head, EXCHANGE: exchange, MERGE: merge, INPUT_GRAD: token_grads, VECTORS: vectors_first, VECTORS_LAST: vectors_last,
    }
    early = [step for step in plan if step[0] in (GRAD_U, GRAD_D)][:3]
    run_plan(early, work, ())
    all_here()
    plan = [step for step in plan if step not in early]
    loops_at = [step[0] for step in plan].index(HEAD_BACK)
    run_plan(plan[:loops_at], work, ())
    ready()
    run_plan(plan[loops_at:], work, ((HEAD_BACK, 2),))
    for i in range(4):
        arrive(pairr.at[i], pr.at[i])
        fin[i, pl.ds(pl.multiple_of(48 * (1 - c), 16), 48), :] = pairr[i]
        D4[i] = fin[i].T
    for w, out in ((0, LO), (1, IG)):
        for m in range(4):
            copies.arrive_or_keep((m == z) & (x == c) & (z // 2 == c), out.at[m], or_.at[w, m], lsem.at[w])
    copies.finish()


def backward_call(plan, chunks, OUT, GF, GC, GST, LOWT, CTX, HID, GI, XO, Q, KT, V, E, CT, RS, WQ, VS):
    n = len(chunks)
    V_ = pltpu.VMEM
    row = (512, 768)
    col = (768, 512)
    sets = [V_((4, 2, 2, 2, 2, 48, 768), BF), V_((2, 2, 4, 48, 3072), BF), V_((2, 2, 2, 2, 48, 3072), BF)]
    return pl.pallas_call(
        partial(backward_kernel, plan, chunks),
        out_shape=[sds((4, 128, 768)), sds((4, 128, 768))] + [sds((4, 192, 96), F32), sds((4, 48, 384), F32), sds((2, 48, 768), F32), sds((16, 384), F32)],
        in_specs=[ANY] * 14 + [VM, ANY, VM],
        out_specs=[ANY, ANY] + [VM] * 4,
        scratch_shapes=sets + sets + [
            V_((512, 3072), BF), V_((512, 3072), BF), V_(col, BF), V_(col, BF), V_((4, 128, 768), BF), V_(row, BF),
            V_((768, 1024), BF), V_((1024, 768), BF), V_(col, BF), V_(row, BF), V_(col, BF), V_(row, F32), V_((2, 1024, 512), BF),
            V_(col, BF), V_((1024, 768), BF), V_((1024, 768), BF), V_(row, BF), V_(row, BF), V_(row, BF), V_((512, 16), F32),
            V_((8, 16, 384), F32), V_((8, 16, 384), F32), V_((16, 384), F32), V_((4, 16, 384), F32), V_((4, 48, 192), F32), V_((4, 48, 192), F32), V_((4, 96, 192), F32),
            S((19,)), S((2,)), S((2,)), S((2,)), S((2,)), S((2, 4)), S((2, 4)), S((n, 5, 8)), S((n, 5, 8)), S((8,)), S((8,)), S((4,)), S((4,)), S((4,)), S((4,)),
        ],
        name="backward",
        compiler_params=pltpu.CompilerParams(collective_id=2, has_side_effects=True, vmem_limit_bytes=59 * 2**20),
    )(OUT, GF, GC, GST, LOWT, CTX, HID, GI, XO, Q, KT, V, E, CT, RS, WQ.reshape(3, 768, 768), VS)


def rows_on_chips(
    inputs, segment_ids, query_weight, query_bias, key_weight, value_weight, value_bias, output_weight, output_bias,
    first_gain, first_shift, up_weight, up_bias, down_weight, down_bias, second_gain, second_shift, cotangent,
):
    small = jnp.stack([query_bias, value_bias, output_bias, first_gain, first_shift, down_bias, second_gain, second_shift])
    kept = forward_call(
        *FORWARD, inputs.reshape(4, 128, 768), cotangent.reshape(4, 128, 768), segment_ids.reshape(4, 1, 128),
        query_weight, key_weight, value_weight, output_weight, up_weight.reshape(4, 48, 384), down_weight.T.reshape(2, 48, 768),
        small, up_bias.reshape(3, 128),
    )
    LO, IG, D4, DU, DD, VO = backward_call(*BACKWARD, *kept)
    v = VO[:8, :96]
    s = (4, 1, 128, 768)
    return (
        LO.reshape(s), IG.reshape(s), D4[0], v[0], D4[1], D4[2], v[1], D4[3], v[2], v[3], v[4], DU.reshape(192, 384), VO[8], DD.reshape(96, 768).T, v[5], v[6], v[7],
    )


EPSILON = 1e-12
NEGATIVE = -1e30


def product(left, right, form):
    return jnp.einsum(form, left, right, preferred_element_type=jnp.float32)


def normalize(hidden, gain, shift):
    centred = hidden - jnp.mean(hidden, axis=-1, keepdims=True)
    scale_inv = lax.rsqrt(jnp.mean(centred * centred, axis=-1, keepdims=True) + EPSILON)
    normed = centred * scale_inv
    return (normed * gain + shift, normed, scale_inv)


def normalize_back(grad_normed, normed, scale_inv):
    centred_grad = grad_normed - jnp.mean(grad_normed, axis=-1, keepdims=True)
    return scale_inv * (
        centred_grad - normed * jnp.mean(grad_normed * normed, axis=-1, keepdims=True)
    )


def same_passage(query_pair, key_pair):
    return jnp.all(query_pair[:, :, None, :] == key_pair[:, None, :, :], axis=-1)[:, None]


def micro_step(shared, tokens, passage_ids, cotan):
    (
        weight_query,
        weight_key,
        weight_value,
        weight_out,
        weight_up,
        weight_down,
        bias_query,
        bias_value,
        bias_out,
        gain_first,
        shift_first,
        bias_up,
        bias_down,
        gain_second,
        shift_second,
    ) = shared
    bias_query = bias_query.astype(jnp.float32)
    bias_value = bias_value.astype(jnp.float32)
    bias_out = bias_out.astype(jnp.float32)
    gain_first = gain_first.astype(jnp.float32)
    shift_first = shift_first.astype(jnp.float32)
    bias_up = bias_up.astype(jnp.float32)
    bias_down = bias_down.astype(jnp.float32)
    gain_second = gain_second.astype(jnp.float32)
    shift_second = shift_second.astype(jnp.float32)
    row_count, seq_count, width = tokens.shape
    token_count = row_count * seq_count
    scale = HD ** (-0.5)
    flat = tokens.reshape(token_count, width)
    queries = (product(flat, weight_query, "md,de->me") + bias_query).astype(jnp.bfloat16)
    keys = product(flat, weight_key, "md,de->me").astype(jnp.bfloat16)
    values = (product(flat, weight_value, "md,de->me") + bias_value).astype(jnp.bfloat16)
    query_four = queries.reshape(row_count, seq_count, HEADS, HD)
    pair_local = jnp.stack((passage_ids // 256, passage_ids % 256), axis=-1).astype(jnp.bfloat16)
    key_rows = keys.reshape(row_count, seq_count, width)
    value_rows = values.reshape(row_count, seq_count, width)
    key_local = key_rows.reshape(row_count, seq_count, HEADS, HD)
    value_local = value_rows.reshape(row_count, seq_count, HEADS, HD)
    running_max = jnp.full((row_count, HEADS, seq_count), NEGATIVE, jnp.float32)
    running_acc = jnp.zeros((row_count, seq_count, HEADS, HD), jnp.float32)
    key_piece = lax.all_gather(key_rows, "blk", axis=1, tiled=True)
    value_piece = lax.all_gather(value_rows, "blk", axis=1, tiled=True)
    pair_piece = lax.all_gather(pair_local, "blk", axis=1, tiled=True)
    count = key_piece.shape[1]
    key_four = key_piece.reshape(row_count, count, HEADS, HD)
    value_four = value_piece.reshape(row_count, count, HEADS, HD)
    allowed = same_passage(pair_local, pair_piece)
    scores = jnp.where(allowed, product(query_four, key_four, "rqhd,rkhd->rhqk") * scale, NEGATIVE)
    fresh_max = jnp.maximum(running_max, jnp.max(scores, axis=-1))
    weights = jnp.where(allowed, jnp.exp(scores - fresh_max[..., None]), 0.0)
    decay = jnp.exp(running_max - fresh_max)
    running_sum = jnp.sum(weights, axis=-1)
    mixed = product(weights.astype(jnp.bfloat16), value_four, "rhqk,rkhd->rqhd")
    running_acc = running_acc * jnp.swapaxes(decay, 1, 2)[..., None] + mixed
    running_max, running_sum, running_acc = (fresh_max, running_sum, running_acc)
    log_total = running_max + jnp.log(running_sum)
    attended = running_acc / jnp.swapaxes(running_sum, 1, 2)[..., None]
    context = attended.reshape(token_count, width).astype(jnp.bfloat16)
    branch = product(context, weight_out, "md,de->me") + bias_out
    first, normed_first, inv_first = normalize(
        flat.astype(jnp.float32) + branch, gain_first, shift_first
    )
    first_low = first.astype(jnp.bfloat16)
    inner = product(first_low, weight_up, "md,df->mf") + bias_up
    activation, gelu_pull = jax.vjp(partial(jax.nn.gelu, approximate=False), inner)
    hidden = activation.astype(jnp.bfloat16)
    second = product(hidden, weight_down, "mf,fd->md") + bias_down
    output, normed_second, inv_second = normalize(first + second, gain_second, shift_second)
    upstream = cotan.reshape(token_count, width).astype(jnp.float32)
    grad_gain_second = jnp.sum(upstream * normed_second, axis=0, keepdims=True)
    grad_shift_second = jnp.sum(upstream, axis=0, keepdims=True)
    grad_sum_second = normalize_back(upstream * gain_second, normed_second, inv_second)
    grad_second = grad_sum_second.astype(jnp.bfloat16)
    grad_weight_down = product(hidden, grad_second, "mf,md->fd")
    grad_bias_down = jnp.sum(grad_second.astype(jnp.float32), axis=0, keepdims=True)
    grad_inner = gelu_pull(product(grad_second, weight_down, "md,fd->mf"))[0].astype(jnp.bfloat16)
    grad_weight_up = product(first_low, grad_inner, "md,mf->df")
    grad_bias_up = jnp.sum(grad_inner.astype(jnp.float32), axis=0, keepdims=True)
    grad_first = grad_sum_second + product(grad_inner, weight_up, "mf,df->md")
    grad_gain_first = jnp.sum(grad_first * normed_first, axis=0, keepdims=True)
    grad_shift_first = jnp.sum(grad_first, axis=0, keepdims=True)
    grad_sum_first = normalize_back(grad_first * gain_first, normed_first, inv_first)
    grad_branch = grad_sum_first.astype(jnp.bfloat16)
    grad_weight_out = product(context, grad_branch, "md,me->de")
    grad_bias_out = jnp.sum(grad_branch.astype(jnp.float32), axis=0, keepdims=True)
    grad_context = product(grad_branch, weight_out, "me,de->md").astype(jnp.bfloat16)
    grad_context_four = grad_context.reshape(row_count, seq_count, HEADS, HD)
    delta = jnp.swapaxes(jnp.sum(grad_context_four.astype(jnp.float32) * attended, axis=-1), 1, 2)
    key_piece = lax.all_gather(key_rows, "blk", axis=1, tiled=True)
    value_piece = lax.all_gather(value_rows, "blk", axis=1, tiled=True)
    pair_piece = lax.all_gather(pair_local, "blk", axis=1, tiled=True)
    count = key_piece.shape[1]
    key_four = key_piece.reshape(row_count, count, HEADS, HD)
    value_four = value_piece.reshape(row_count, count, HEADS, HD)
    allowed = same_passage(pair_local, pair_piece)
    scores = jnp.where(allowed, product(query_four, key_four, "rqhd,rkhd->rhqk") * scale, NEGATIVE)
    probs = jnp.where(allowed, jnp.exp(scores - log_total[..., None]), 0.0)
    grad_probs = product(grad_context_four, value_four, "rqhd,rkhd->rhqk")
    grad_scores = (probs * (grad_probs - delta[..., None])).astype(jnp.bfloat16)
    grad_query_acc = product(grad_scores, key_four, "rhqk,rkhd->rqhd") * scale
    grad_queries = grad_query_acc.reshape(token_count, width).astype(jnp.bfloat16)
    pair_wide = pair_local.astype(jnp.float32)
    sent = (
        queries.reshape(row_count, seq_count, width).astype(jnp.float32),
        grad_context.reshape(row_count, seq_count, width).astype(jnp.float32),
        jnp.swapaxes(log_total, 1, 2),
        jnp.swapaxes(delta, 1, 2),
        pair_wide,
    )
    query_piece = lax.all_gather(sent[0], "blk", axis=1, tiled=True)
    context_piece = lax.all_gather(sent[1], "blk", axis=1, tiled=True)
    total_piece = lax.all_gather(sent[2], "blk", axis=1, tiled=True)
    delta_piece = lax.all_gather(sent[3], "blk", axis=1, tiled=True)
    pair_piece = lax.all_gather(sent[4], "blk", axis=1, tiled=True)
    count = query_piece.shape[1]
    query_part = query_piece.astype(jnp.bfloat16).reshape(row_count, count, HEADS, HD)
    context_part = context_piece.astype(jnp.bfloat16).reshape(row_count, count, HEADS, HD)
    total_part = jnp.swapaxes(total_piece, 1, 2)
    delta_part = jnp.swapaxes(delta_piece, 1, 2)
    allowed = same_passage(pair_piece, pair_wide)
    scores = jnp.where(allowed, product(query_part, key_local, "rqhd,rkhd->rhqk") * scale, NEGATIVE)
    probs = jnp.where(allowed, jnp.exp(scores - total_part[..., None]), 0.0)
    grad_value_acc = product(probs.astype(jnp.bfloat16), context_part, "rhqk,rqhd->rkhd")
    grad_probs = product(context_part, value_local, "rqhd,rkhd->rhqk")
    grad_scores = (probs * (grad_probs - delta_part[..., None])).astype(jnp.bfloat16)
    grad_key_acc = product(grad_scores, query_part, "rhqk,rqhd->rkhd") * scale
    grad_key_acc, grad_value_acc = (grad_key_acc, grad_value_acc)
    grad_keys = grad_key_acc.reshape(token_count, width).astype(jnp.bfloat16)
    grad_values = grad_value_acc.reshape(token_count, width).astype(jnp.bfloat16)
    grad_weight_query = product(flat, grad_queries, "md,me->de")
    grad_bias_query = jnp.sum(grad_queries.astype(jnp.float32), axis=0, keepdims=True)
    grad_weight_key = product(flat, grad_keys, "md,me->de")
    grad_weight_value = product(flat, grad_values, "md,me->de")
    grad_bias_value = jnp.sum(grad_values.astype(jnp.float32), axis=0, keepdims=True)
    grad_tokens = (
        grad_sum_first
        + product(grad_queries, weight_query, "me,de->md")
        + product(grad_keys, weight_key, "me,de->md")
        + product(grad_values, weight_value, "me,de->md")
    )
    contributions = (
        grad_weight_query,
        grad_weight_key,
        grad_weight_value,
        grad_weight_out,
        grad_weight_up,
        grad_weight_down,
        grad_bias_query,
        grad_bias_value,
        grad_bias_out,
        grad_gain_first,
        grad_shift_first,
        grad_bias_up,
        grad_bias_down,
        grad_gain_second,
        grad_shift_second,
    )
    return (
        output.astype(jnp.bfloat16).reshape(row_count, seq_count, width),
        grad_tokens.astype(jnp.bfloat16).reshape(row_count, seq_count, width),
        contributions,
    )


def general(
    inputs,
    segment_ids,
    query_weight,
    query_bias,
    key_weight,
    value_weight,
    value_bias,
    output_weight,
    output_bias,
    first_gain,
    first_shift,
    up_weight,
    up_bias,
    down_weight,
    down_bias,
    second_gain,
    second_shift,
    cotangent,
):
    outputs = []
    input_grads = []
    totals = None
    widened = (
        lax.all_gather(query_weight, "blk", axis=1, tiled=True),
        lax.all_gather(key_weight, "blk", axis=1, tiled=True),
        lax.all_gather(value_weight, "blk", axis=1, tiled=True),
        lax.all_gather(output_weight, "blk", axis=1, tiled=True),
        lax.all_gather(up_weight, "blk", axis=1, tiled=True),
        lax.all_gather(down_weight, "blk", axis=1, tiled=True),
        lax.all_gather(query_bias.reshape(1, -1), "blk", axis=1, tiled=True),
        lax.all_gather(value_bias.reshape(1, -1), "blk", axis=1, tiled=True),
        lax.all_gather(output_bias.reshape(1, -1), "blk", axis=1, tiled=True),
        lax.all_gather(first_gain.reshape(1, -1), "blk", axis=1, tiled=True),
        lax.all_gather(first_shift.reshape(1, -1), "blk", axis=1, tiled=True),
        lax.all_gather(up_bias.reshape(1, -1), "blk", axis=1, tiled=True),
        lax.all_gather(down_bias.reshape(1, -1), "blk", axis=1, tiled=True),
        lax.all_gather(second_gain.reshape(1, -1), "blk", axis=1, tiled=True),
        lax.all_gather(second_shift.reshape(1, -1), "blk", axis=1, tiled=True),
    )
    complete = (
        lax.all_gather(widened[0], "dp", axis=0, tiled=True),
        lax.all_gather(widened[1], "dp", axis=0, tiled=True),
        lax.all_gather(widened[2], "dp", axis=0, tiled=True),
        lax.all_gather(widened[3], "dp", axis=0, tiled=True),
        lax.all_gather(widened[4], "dp", axis=0, tiled=True),
        lax.all_gather(widened[5], "dp", axis=0, tiled=True),
    )
    shared = tuple(complete) + tuple(widened[6:])
    for batch_index in range(inputs.shape[0]):
        layer_out, layer_grad, contributions = micro_step(
            shared, inputs[batch_index], segment_ids[batch_index], cotangent[batch_index]
        )
        outputs.append(layer_out)
        input_grads.append(layer_grad)
        if totals is None:
            totals = contributions
        else:
            totals = tuple((earlier + latest for earlier, latest in zip(totals, contributions)))
    narrowed = (
        lax.psum_scatter(totals[0], "blk", scatter_dimension=1, tiled=True),
        lax.psum_scatter(totals[1], "blk", scatter_dimension=1, tiled=True),
        lax.psum_scatter(totals[2], "blk", scatter_dimension=1, tiled=True),
        lax.psum_scatter(totals[3], "blk", scatter_dimension=1, tiled=True),
        lax.psum_scatter(totals[4], "blk", scatter_dimension=1, tiled=True),
        lax.psum_scatter(totals[5], "blk", scatter_dimension=1, tiled=True),
        lax.psum_scatter(totals[6], "blk", scatter_dimension=1, tiled=True),
        lax.psum_scatter(totals[7], "blk", scatter_dimension=1, tiled=True),
        lax.psum_scatter(totals[8], "blk", scatter_dimension=1, tiled=True),
        lax.psum_scatter(totals[9], "blk", scatter_dimension=1, tiled=True),
        lax.psum_scatter(totals[10], "blk", scatter_dimension=1, tiled=True),
        lax.psum_scatter(totals[11], "blk", scatter_dimension=1, tiled=True),
        lax.psum_scatter(totals[12], "blk", scatter_dimension=1, tiled=True),
        lax.psum_scatter(totals[13], "blk", scatter_dimension=1, tiled=True),
        lax.psum_scatter(totals[14], "blk", scatter_dimension=1, tiled=True),
    )
    matrix_sums = (
        lax.psum_scatter(narrowed[0], "dp", scatter_dimension=0, tiled=True),
        lax.psum_scatter(narrowed[1], "dp", scatter_dimension=0, tiled=True),
        lax.psum_scatter(narrowed[2], "dp", scatter_dimension=0, tiled=True),
        lax.psum_scatter(narrowed[3], "dp", scatter_dimension=0, tiled=True),
        lax.psum_scatter(narrowed[4], "dp", scatter_dimension=0, tiled=True),
        lax.psum_scatter(narrowed[5], "dp", scatter_dimension=0, tiled=True),
    )
    vector_sums = lax.psum(
        (
            narrowed[6],
            narrowed[7],
            narrowed[8],
            narrowed[9],
            narrowed[10],
            narrowed[11],
            narrowed[12],
            narrowed[13],
            narrowed[14],
        ),
        "dp",
    )
    return (
        jnp.stack(outputs),
        jnp.stack(input_grads),
        matrix_sums[0],
        vector_sums[0].reshape(-1),
        matrix_sums[1],
        matrix_sums[2],
        vector_sums[1].reshape(-1),
        matrix_sums[3],
        vector_sums[2].reshape(-1),
        vector_sums[3].reshape(-1),
        vector_sums[4].reshape(-1),
        matrix_sums[4],
        vector_sums[5].reshape(-1),
        matrix_sums[5],
        vector_sums[6].reshape(-1),
        vector_sums[7].reshape(-1),
        vector_sums[8].reshape(-1),
    )


def solution(mesh):
    in_specs = (
        P(None, "dp", "blk", None),
        P(None, "dp", "blk"),
        P("dp", "blk"),
        P("blk"),
        P("dp", "blk"),
        P("dp", "blk"),
        P("blk"),
        P("dp", "blk"),
        P("blk"),
        P("blk"),
        P("blk"),
        P("dp", "blk"),
        P("blk"),
        P("dp", "blk"),
        P("blk"),
        P("blk"),
        P("blk"),
        P(None, "dp", "blk", None),
    )
    out_specs = (
        P(None, "dp", "blk", None),
        P(None, "dp", "blk", None),
        P("dp", "blk"),
        P("blk"),
        P("dp", "blk"),
        P("dp", "blk"),
        P("blk"),
        P("dp", "blk"),
        P("blk"),
        P("blk"),
        P("blk"),
        P("dp", "blk"),
        P("blk"),
        P("dp", "blk"),
        P("blk"),
        P("blk"),
        P("blk"),
    )
    small = mesh.shape["dp"] == 4 and mesh.shape["blk"] == 8

    def on_device(*arrays):
        if small and arrays[0].shape == (4, 1, 128, 768):
            return rows_on_chips(*arrays)
        return general(*arrays)

    return jax.shard_map(
        on_device, mesh=mesh, in_specs=in_specs, out_specs=out_specs, check_vma=False
    )
```

profile of v0, /device:TPU:1, one launch (start us, length us, event | category | flops | bytes accessed | tf_op | source)
XLA Modules:
  0.0 232.8 jit_solution(15033950896456351048)
XLA Ops:
  0.7 1.4 stack.35.small
  2.0 121.1 %forward.1 = (bf16[512,768]{1,0:T(8,128)(2,1)}, f32[512,768]{1,0:T(8,128)}, bf16[512,768]{1,0:T(8,128)(2,1)}, bf16[768,512]{1,0:T(8,128)(2,1)}, bf16[768,512]{1,...) custom-call(bf16[4,128,768]{2,1,0:T(8,128)(2,1)} %bitcast.51, ...), custom_call_target="tpu_custom_call" | custom-call | tf_op jit(solution)/shard_map/forward/pallas_call | solution.py:498
  123.1 99.4 %backward.1 = (bf16[4,128,768]{2,1,0:T(8,128)(2,1)}, bf16[4,128,768]{2,1,0:T(8,128)(2,1)}, f32[4,192,96]{2,1,0:T(8,128)}, f32[4,48,384]{2,1,0:T(8,128)}, f32[2,48,768]{2,1,0:T(8,128)}, /*index=5*/f32[16,384]{1,0:T(8,128)}) custom-call(bf16[512,768]{1,0:T(8,128)(2,1)} %get-tuple-element.40.OUT, f32[512,768]{1,0:T(8,128)} %get-tuple-element.41.GF, ...), custom_call_target="tpu_custom_call" | custom-call | tf_op jit(solution)/shard_map/backward/pallas_call | solution.py:782
  222.5 0.0 copy-start.1
  222.5 0.0 copy-start
  222.5 1.4 slice_reduce_fusion
  223.9 1.5 slice_bitcast_fusion.4
  225.4 1.8 slice_bitcast_fusion
  227.2 2.1 copy.41
  229.3 2.1 copy.42
  231.3 0.0 copy-done.1
  231.3 0.7 copy.43
  232.0 0.0 copy-done
  232.0 0.7 copy.44
Async XLA Ops:
  222.5 8.8 %copy-start.1 = (f32[4,48,384]{2,1,0:T(8,128)S(1)}, f32[4,48,384]{2,1,0:T(8,128)}, u32[]{:S(2)}) copy-start(f32[4,48,384]{2,1,0:T(8,128)} %get-tuple-element.61) | copy-start | bytes 884740
  222.5 9.5 %copy-start = (f32[2,48,768]{2,1,0:T(8,128)S(1)}, f32[2,48,768]{2,1,0:T(8,128)}, u32[]{:S(2)}) copy-start(f32[2,48,768]{2,1,0:T(8,128)} %get-tuple-element.62) | copy-start | bytes 884740
where the time goes:
time: 235 us; the launch traced here: 233 us
  Pallas kernels  220 us (94%)
  local copies, waits for them, and re-layouts  11.6 us (5%)
    pallas_call x1, Pallas kernels, forward_call(): pl.pallas_call(partial(forward_kernel, plan, chunks), out_shape=[sds(row)...  121 us
    pallas_call x1, Pallas kernels, backward_call(): pl.pallas_call(partial(backward_kernel, plan, chunks), out_shape=[sds((4,...  99.4 us
    unnamed x8, local copies, waits for them, and re-layouts  5.56 us

commit v1 on v0

--- a/solution.py
+++ b/solution.py
@@ -129,22 +129,22 @@
     (RELAY, 10, 3), (RELAY, 11, 3), (RELAY, 10, 4), (RELAY, 11, 4), (DOWN, 1),
 )
 BACKWARD_CHUNKS = (
-    ("d", 3, "bxayc"), ("d", 0, "axbyc"), ("u", 3, "axybc"), ("d", 1, "abyxc"), ("d", 2, "aybxc"), ("u", 1, "bxayc"), ("u", 2, "baxyc"),
-    ("t", 3, "aybxc"), ("u", 0, "baxyc"), ("t", 0, "abxyc"), ("t", 1, "baxyc"), ("t", 2, "axbyc"),
+    ("d", 2, "axbyc"), ("d", 0, "abxyc"), ("d", 3, "byaxc"), ("u", 0, "axbyc"), ("u", 3, "bxayc"), ("t", 3, "yabxc"), ("u", 2, "axbyc"),
+    ("u", 1, "abyxc"), ("d", 1, "axbyc"), ("t", 2, "axbyc"), ("t", 0, "baxyc"), ("t", 1, "abxyc"),
 )
 BACKWARD_PLAN = (
-    (GRAD_D, 3), (LAUNCH, 0), (GRAD_D, 0), (LAUNCH, 1), (HOME, 0), (HOME, 1), (HOME, 2), (HEAD_BACK, 0), (ABSORB, 0, 0), (GRAD_U, 3),
-    (LAUNCH, 2), (ABSORB, 1, 0), (GRAD_D, 1), (LAUNCH, 3), (HOME, 3), (HEAD_BACK, 1), (ABSORB, 2, 0), (GRAD_D, 2), (LAUNCH, 4),
-    (ABSORB, 0, 1), (ABSORB, 3, 0), (GRAD_U, 1), (LAUNCH, 5), (HEAD_BACK, 2), (ABSORB, 4, 0), (GRAD_U, 2), (LAUNCH, 6), (ABSORB, 1, 1),
-    (ABSORB, 5, 0), (GRAD_T, 3), (LAUNCH, 7), (HEAD_BACK, 3), (ABSORB, 6, 0), (GRAD_U, 0), (LAUNCH, 8), (ABSORB, 3, 1), (ABSORB, 7, 0),
-    (ABSORB, 2, 1), (ABSORB, 5, 1), (HEAD_BACK, 4), (ABSORB, 8, 0), (HEAD_BACK, 5), (HEAD_BACK, 6), (ABSORB, 4, 1), (ABSORB, 6, 1),
-    (HEAD_BACK, 7), (HEAD_BACK, 8), (ABSORB, 0, 2), (ABSORB, 1, 2), (HEAD_BACK, 9), (ABSORB, 3, 2), (ABSORB, 7, 1), (HEAD_BACK, 10),
-    (HEAD_BACK, 11), (EXCHANGE,), (ABSORB, 2, 2), (ABSORB, 4, 2), (ABSORB, 3, 3), (ABSORB, 5, 2), (ABSORB, 6, 2), (ABSORB, 8, 1),
-    (ABSORB, 0, 3), (ABSORB, 7, 2), (ABSORB, 1, 3), (MERGE,), (GRAD_T, 0), (LAUNCH, 9), (ABSORB, 2, 3), (ABSORB, 3, 4), (GRAD_T, 1),
-    (LAUNCH, 10), (ABSORB, 0, 4), (ABSORB, 4, 3), (ABSORB, 5, 3), (INPUT_GRAD,), (ABSORB, 6, 3), (ABSORB, 1, 4), (ABSORB, 7, 3),
-    (ABSORB, 8, 2), (ABSORB, 9, 0), (ABSORB, 10, 0), (ABSORB, 2, 4), (GRAD_T, 2), (LAUNCH, 11), (ABSORB, 5, 4), (ABSORB, 4, 4),
-    (ABSORB, 11, 0), (ABSORB, 9, 1), (ABSORB, 10, 1), (ABSORB, 6, 4), (ABSORB, 11, 1), (ABSORB, 9, 2), (ABSORB, 7, 4), (ABSORB, 10, 2),
-    (ABSORB, 8, 3), (VECTORS,), (ABSORB, 11, 2), (ABSORB, 9, 3), (ABSORB, 8, 4), (ABSORB, 11, 3), (ABSORB, 10, 3), (ABSORB, 9, 4),
+    (GRAD_D, 2), (LAUNCH, 0), (GRAD_D, 0), (LAUNCH, 1), (HOME, 0), (HOME, 1), (HEAD_BACK, 0), (ABSORB, 0, 0), (GRAD_D, 3), (LAUNCH, 2),
+    (ABSORB, 1, 0), (GRAD_U, 0), (LAUNCH, 3), (HOME, 2), (HOME, 3), (HEAD_BACK, 1), (ABSORB, 2, 0), (GRAD_U, 3), (LAUNCH, 4),
+    (ABSORB, 0, 1), (ABSORB, 3, 0), (GRAD_T, 3), (LAUNCH, 5), (HEAD_BACK, 2), (ABSORB, 4, 0), (GRAD_U, 2), (LAUNCH, 6), (ABSORB, 1, 1),
+    (ABSORB, 5, 0), (GRAD_U, 1), (LAUNCH, 7), (HEAD_BACK, 3), (ABSORB, 6, 0), (GRAD_D, 1), (LAUNCH, 8), (ABSORB, 2, 1), (ABSORB, 3, 1),
+    (ABSORB, 0, 2), (ABSORB, 7, 0), (HEAD_BACK, 4), (ABSORB, 8, 0), (HEAD_BACK, 5), (HEAD_BACK, 6), (ABSORB, 1, 2), (ABSORB, 4, 1),
+    (HEAD_BACK, 7), (ABSORB, 3, 2), (ABSORB, 5, 1), (HEAD_BACK, 8), (ABSORB, 1, 3), (ABSORB, 2, 2), (HEAD_BACK, 9), (ABSORB, 0, 3),
+    (ABSORB, 6, 1), (HEAD_BACK, 10), (HEAD_BACK, 11), (EXCHANGE,), (ABSORB, 7, 1), (ABSORB, 5, 2), (ABSORB, 8, 1), (ABSORB, 4, 2),
+    (ABSORB, 1, 4), (ABSORB, 3, 3), (ABSORB, 0, 4), (MERGE,), (GRAD_T, 2), (LAUNCH, 9), (ABSORB, 2, 3), (ABSORB, 4, 3), (ABSORB, 6, 2),
+    (GRAD_T, 0), (LAUNCH, 10), (INPUT_GRAD,), (ABSORB, 5, 3), (ABSORB, 7, 2), (ABSORB, 6, 3), (ABSORB, 8, 2), (ABSORB, 9, 0),
+    (ABSORB, 2, 4), (ABSORB, 10, 0), (ABSORB, 4, 4), (ABSORB, 3, 4), (GRAD_T, 1), (LAUNCH, 11), (ABSORB, 5, 4), (ABSORB, 11, 0),
+    (ABSORB, 9, 1), (ABSORB, 10, 1), (ABSORB, 8, 3), (ABSORB, 11, 1), (ABSORB, 7, 3), (ABSORB, 10, 2), (ABSORB, 6, 4), (ABSORB, 9, 2),
+    (ABSORB, 11, 2), (VECTORS,), (ABSORB, 8, 4), (ABSORB, 7, 4), (ABSORB, 9, 3), (ABSORB, 11, 3), (ABSORB, 10, 3), (ABSORB, 9, 4),
     (ABSORB, 10, 4), (ABSORB, 11, 4), (VECTORS_LAST,),
 )
 FORWARD = (FORWARD_PLAN, FORWARD_CHUNKS)
@@ -225,7 +225,7 @@
 
 def forward_kernel(
     plan, chunks,
-    xs, cot, seg, qw, kw, vw, ow, wup, wdt, small, upb,
+    xs, cot, seg, qw, kw, vw, ow, wup, wdt, upb, s0, s1, s2, s3, s4, s5, s6, s7,
     OUT, GF, GC, GST, LOWT, CTX, HID, GI, XO, Q, KT, V, E, CT, RS, WQ, VS,
     wt, wu, wd, pair_src, pair_dst, stage, xbuf, cbuf, sbuf, vec, vbuf, vb, ub,
     qb, kb, ktb, vb_, vtb, mask, ebuf, ctb, rsb, vsb, hid, gib, ctxb, n1, first, acc, rowbuf, outb, gsb, lowb, gcb, gsn,
@@ -247,7 +247,8 @@
     for i, w in enumerate((qw, kw, vw, ow)):
         pair_src[i] = w[...].astype(F32).T.astype(BF)
     vec[...] = jnp.zeros_like(vec)
-    vec[0:8, 0:96] = small[...].astype(F32)
+    for i, v in enumerate((s0, s1, s2, s3, s4, s5, s6, s7)):
+        vec[i : i + 1, 0:96] = v[...].astype(F32)
     vec[8:11, :] = upb[...].astype(F32)
     greet_all()()
     copies.start(lambda: (pair_src.at[:, pl.ds(48 * (1 - c), 48)], pair_dst, ps, pr, partner))
@@ -502,7 +503,7 @@
             sds((4, 128, 768)), sds(row), sds((768, 1024)), sds((1024, 768)), sds((12, 1024, 512)), sds((768, 512)), sds((16, 512), F32),
             sds((3, 2, 2, 2, 2, 48, 768)), sds((16, 3072), F32),
         ],
-        in_specs=[ANY, ANY] + [VM] * 9,
+        in_specs=[ANY, ANY] + [VM] * 16,
         out_specs=[ANY] * 16 + [VM],
         scratch_shapes=[
             V_((4, 2, 2, 2, 2, 48, 768), BF), V_((2, 2, 4, 48, 3072), BF), V_((2, 2, 2, 2, 48, 3072), BF),
@@ -516,7 +517,7 @@
         ],
         name="forward",
         compiler_params=pltpu.CompilerParams(collective_id=1, has_side_effects=True, vmem_limit_bytes=59 * 2**20),
-    )(xs, cot, seg, qw, kw, vw, ow, wup, wdt, small, upb)
+    )(xs, cot, seg, qw, kw, vw, ow, wup, wdt, upb, *small)
 
 
 def landing(at, order, s):
@@ -659,12 +660,13 @@
         if i == 3:
             need("gf", "ctx")
             gt[3] = dot(gfb[...].T.astype(BF), igb[...]).astype(BF).reshape(shape)
-        elif i == 0:
-            need("x")
-            gt[0] = dot(dqt[...], xb[...].reshape(512, 768)).astype(BF).reshape(shape)
+            return
+        need("x")
+        if i == 0:
+            left = dqt[...]
         else:
-            src = dkr if i == 1 else dvr
-            gt[i] = dot(src[...].astype(F32).T.astype(BF), xb[...].reshape(512, 768)).astype(BF).reshape(shape)
+            left = (dkr if i == 1 else dvr)[...].astype(F32).T.astype(BF)
+        gt[i] = dot(left, xb[...].reshape(512, 768)).astype(BF).reshape(shape)
 
     def ready():
         need("gc", "v", "q", "kt", "ct")
@@ -796,21 +798,50 @@
     )(OUT, GF, GC, GST, LOWT, CTX, HID, GI, XO, Q, KT, V, E, CT, RS, WQ.reshape(3, 768, 768), VS)
 
 
+def finish_kernel(lo, ig, d4, du, dd, vo, LO, IG, DQ, DK, DV, DO, DU, DD, *rest):
+    rows, held, (sem_in, sem_out) = rest[:9], rest[9:17], rest[17:]
+    pairs = [(lo, LO), (ig, IG), (du, DU), (dd, DD)] + [(d4.at[i], out) for i, out in enumerate((DQ, DK, DV, DO))]
+    taken = [pltpu.make_async_copy(src, buf, sem_in.at[i]) for i, ((src, _), buf) in enumerate(zip(pairs, held))]
+    given = [pltpu.make_async_copy(buf, dst, sem_out.at[i]) for i, ((_, dst), buf) in enumerate(zip(pairs, held))]
+    for cp in taken:
+        cp.start()
+    for i, row in enumerate(rows):
+        row[...] = vo[i : i + 1, : row.shape[1]]
+    for one, other in zip(taken, given):
+        one.wait()
+        other.start()
+    for cp in given:
+        cp.wait()
+
+
+def finish_call(lo, ig, d4, du, dd, vo):
+    return pl.pallas_call(
+        finish_kernel,
+        out_shape=[sds((4, 128, 768)), sds((4, 128, 768))] + [sds((192, 96), F32)] * 4 + [sds((4, 48, 384), F32), sds((2, 48, 768), F32)]
+        + [sds((1, 96), F32)] * 8 + [sds((1, 384), F32)],
+        in_specs=[ANY] * 5 + [VM],
+        out_specs=[ANY] * 8 + [VM] * 9,
+        scratch_shapes=[pltpu.VMEM((4, 128, 768), BF)] * 2 + [pltpu.VMEM((4, 48, 384), F32), pltpu.VMEM((2, 48, 768), F32)] + [pltpu.VMEM((192, 96), F32)] * 4
+        + [pltpu.SemaphoreType.DMA((8,))] * 2,
+        name="finish",
+    )(lo, ig, d4, du, dd, vo)
+
+
 def rows_on_chips(
     inputs, segment_ids, query_weight, query_bias, key_weight, value_weight, value_bias, output_weight, output_bias,
     first_gain, first_shift, up_weight, up_bias, down_weight, down_bias, second_gain, second_shift, cotangent,
 ):
-    small = jnp.stack([query_bias, value_bias, output_bias, first_gain, first_shift, down_bias, second_gain, second_shift])
+    small = [v.reshape(1, 96) for v in (query_bias, value_bias, output_bias, first_gain, first_shift, down_bias, second_gain, second_shift)]
     kept = forward_call(
         *FORWARD, inputs.reshape(4, 128, 768), cotangent.reshape(4, 128, 768), segment_ids.reshape(4, 1, 128),
         query_weight, key_weight, value_weight, output_weight, up_weight.reshape(4, 48, 384), down_weight.T.reshape(2, 48, 768),
         small, up_bias.reshape(3, 128),
     )
-    LO, IG, D4, DU, DD, VO = backward_call(*BACKWARD, *kept)
-    v = VO[:8, :96]
+    LO, IG, DQ, DK, DV, DO, DU, DD, *v = finish_call(*backward_call(*BACKWARD, *kept))
+    v = [row.reshape(-1) for row in v]
     s = (4, 1, 128, 768)
     return (
-        LO.reshape(s), IG.reshape(s), D4[0], v[0], D4[1], D4[2], v[1], D4[3], v[2], v[3], v[4], DU.reshape(192, 384), VO[8], DD.reshape(96, 768).T, v[5], v[6], v[7],
+        LO.reshape(s), IG.reshape(s), DQ, v[0], DK, DV, v[1], DO, v[2], v[3], v[4], DU.reshape(192, 384), v[8], DD.reshape(96, 768).T, v[5], v[6], v[7],
     )
 
 

time: 235 us -> 227 us (0.966); the launches traced: 233 us -> 227 us
  local copies, waits for them, and re-layouts: 11.6 us -> 0 us
  Pallas kernels: 220 us -> 225 us
    unnamed x8 -> x0, local copies, waits for them, and re-layouts: 5.56 us -> none
    pallas_call x0 -> x1, Pallas kernels: none -> 4.1 us  [finish_call(): pl.pallas_call(finish_kernel, out_shape=[sds((4, 128, 768)), sds((4, 128,...]
    squeeze x2 -> x0, local copies, waits for them, and re-layouts: 3.29 us -> none  [the longest x1 1.78 us: rows_on_chips(): D4[3]]
where the time goes in v1:
time: 227 us
  Pallas kernels  225 us (99%)
    pallas_call x1, Pallas kernels, forward_call(): pl.pallas_call(partial(forward_kernel, plan, chunks), out_shape=[sds(row)...  121 us
    pallas_call x1, Pallas kernels, backward_call(): pl.pallas_call(partial(backward_kernel, plan, chunks), out_shape=[sds((4,...  99.9 us

profile of v1, /device:TPU:1, one launch (start us, length us, event | category | flops | bytes accessed | tf_op | source)
XLA Modules:
  0.0 227.2 jit_solution(17792685797699408053)
XLA Ops:
  0.7 121.3 %forward.1 = (bf16[512,768]{1,0:T(8,128)(2,1)}, f32[512,768]{1,0:T(8,128)}, bf16[512,768]{1,0:T(8,128)(2,1)}, bf16[768,512]{1,0:T(8,128)(2,1)}, bf16[768,512]{1,...) custom-call(bf16[4,128,768]{2,1,0:T(8,128)(2,1)} %bitcast.35, ...), custom_call_target="tpu_custom_call" | custom-call | tf_op jit(solution)/shard_map/forward/pallas_call | solution.py:499
  121.9 99.9 %backward.1 = (bf16[4,128,768]{2,1,0:T(8,128)(2,1)}, bf16[4,128,768]{2,1,0:T(8,128)(2,1)}, f32[4,192,96]{2,1,0:T(8,128)}, f32[4,48,384]{2,1,0:T(8,128)}, f32[2,48,768]{2,1,0:T(8,128)}, /*index=5*/f32[16,384]{1,0:T(8,128)}) custom-call(bf16[512,768]{1,0:T(8,128)(2,1)} %get-tuple-element.57.OUT, f32[512,768]{1,0:T(8,128)} %get-tuple-element.58.GF, ...), custom_call_target="tpu_custom_call" | custom-call | tf_op jit(solution)/shard_map/backward/pallas_call | solution.py:784
  221.8 4.1 %finish.1 = (bf16[4,128,768]{2,1,0:T(8,128)(2,1)}, bf16[4,128,768]{2,1,0:T(8,128)(2,1)}, f32[192,96]{1,0:T(8,128)}, f32[192,96]{1,0:T(8,128)}, f32[192,96]{1,0:T...) custom-call(bf16[4,128,768]{2,1,0:T(8,128)(2,1)} %get-tuple-element., ...), custom_call_target="tpu_custom_call" | custom-call | tf_op jit(solution)/shard_map/finish/pallas_call | solution.py:818
  225.9 1.3 reduce
